TPU v7x, 32 devices: a whole 2x2x4 slice. The times are simulated.
32 devices in a mesh: filt: 4 (over z), space: 8 (over y, x, core).
Axes of the slice: x: 2, y: 2, z: 4, core: 2. Of those that a mesh axis runs over, the one named last changes fastest.
Arguments:
- inputs: bfloat16 [8, 256, 2048], P('space', 'filt'), may hold values from -6 to 6
- weight: bfloat16 [3, 3, 3, 256, 256], P(None, None, None, 'filt'), may hold values from -0.078125 to 0.078125
- bias: bfloat16 [256], P('filt'), may hold values from -4 to 4
- cotangent: bfloat16 [8, 256, 2048], P('space', 'filt'), may hold values from -6 to 6
Outputs:
- output: float32 [8, 256, 2048], P('space', 'filt')
- grad_inputs: float32 [8, 256, 2048], P('space', 'filt')
- grad_weight: float32 [3, 3, 3, 256, 256], P(None, None, None, 'filt')
- grad_bias: float32 [256], P('filt')
All inputs are finite; a program needn't handle non-finite values.
Results may differ from a plain program's by a relative error of at most 0.0003.
Values may be sent and summed in bfloat16 or wider, within the bound.
A program may use at most 64 MiB of HBM per device.

v0:
```python
import functools

import jax
import jax.numpy as jnp
from jax import lax
from jax.experimental import pallas as pl
from jax.experimental.pallas import tpu as pltpu
from jax.sharding import PartitionSpec as P

ROWS = 32
WIDE = 64
TILE = 512
BF16 = jnp.bfloat16
F32 = jnp.float32


def remote(src, dst, send_sem, recv_sem, **where):
    return pltpu.make_async_remote_copy(
        src_ref=src,
        dst_ref=dst,
        send_sem=send_sem,
        recv_sem=recv_sem,
        device_id=where,
        device_id_type=pl.DeviceIdType.MESH,
    )


def kernel(
    F, S, Q, factor,
    in_ref, w_ref, bias_ref, cot_ref,
    out_ref, gi_ref, gw_ref, gb_ref,
    xin, xcot, in3, s_cot, s_in, wst, wrx, wf,
    hs_b, hr_b, hs_f, hr_f, grad, gpair, grx, gfin,
    cot_ss, cot_rs, in_ss, in_rs, halo_ss, halo_rs,
    w1_ss, w1_rs, w2_ss, w2_rs,
    hb_ss, hb_rs, hf_ss, hf_rs,
    pair_ss, pair_rs, rs_ss, rs_rs, ag_ss, ag_rs, lo_ss, lo_rs,
):
    f = lax.axis_index("filt")
    s = lax.axis_index("space")
    cf, plane = in_ref.shape
    chans = w_ref.shape[2]
    half = chans // 2
    H = S // 2
    core = lax.rem(s, 2)
    chip = s // 2
    partner = s + 1 - 2 * core
    tiles = plane // TILE

    barrier = pltpu.get_barrier_semaphore()
    for d in range(1, F):
        pl.semaphore_signal(barrier, inc=1, device_id={"filt": lax.rem(f + d, F)},
                            device_id_type=pl.DeviceIdType.MESH)
    for d in range(1, S):
        pl.semaphore_signal(barrier, inc=1, device_id={"space": lax.rem(s + d, S)},
                            device_id_type=pl.DeviceIdType.MESH)
    pl.semaphore_wait(barrier, F - 1 + S - 1)

    def line(own, buf, ss, rs, t, way):
        shard = f - (t - 1) if way == 0 else f + (t - 1)
        src = own if t == 1 else buf.at[shard]
        to = f + 1 if way == 0 else f - 1
        return remote(src, buf.at[shard], ss.at[way, t - 1], rs.at[way, t - 1], filt=to)

    def sends(t, way):
        if way == 0:
            return jnp.logical_and(f - (t - 1) >= 0, f + 1 < F)
        return jnp.logical_and(f + (t - 1) < F, f - 1 >= 0)

    def arrives(t, way):
        return f - t >= 0 if way == 0 else f + t < F

    def start_line(own, buf, ss, rs):
        for way in range(2):
            @pl.when(sends(1, way))
            def _():
                line(own, buf, ss, rs, 1, way).start()

    def relay(own, buf, ss, rs, t):
        for way in range(2):
            @pl.when(arrives(t, way))
            def _():
                shard = f - t if way == 0 else f + t
                remote(own, buf.at[shard], ss.at[way, t - 1], rs.at[way, t - 1],
                       filt=lax.rem(f + 1, F)).wait_recv()
            if t + 1 < F:
                @pl.when(sends(t + 1, way))
                def _():
                    line(own, buf, ss, rs, t + 1, way).start()

    def end_line(own, buf, ss, rs):
        for way in range(2):
            for t in range(1, F):
                @pl.when(sends(t, way))
                def _():
                    line(own, buf, ss, rs, t, way).wait_send()

    lane = lax.broadcasted_iota(jnp.int32, (16, plane), 1)
    col = lax.rem(lane, WIDE)

    def build(src, row0, dst):
        def step(c, _):
            at = pl.multiple_of(c * 16, 16)
            x = src[pl.ds(at, 16), :].astype(F32)
            to = pl.multiple_of(row0 + c * 16, 16)
            for jw in range(3):
                y = x
                if jw == 0:
                    y = jnp.where(col < WIDE - 1, pltpu.roll(x, plane - 1, 1), 0.0)
                if jw == 2:
                    y = jnp.where(col > 0, pltpu.roll(x, 1, 1), 0.0)
                for jr in range(3):
                    z = y
                    if jr == 0:
                        z = jnp.where(lane < plane - WIDE, pltpu.roll(y, plane - WIDE, 1), 0.0)
                    if jr == 2:
                        z = jnp.where(lane >= WIDE, pltpu.roll(y, WIDE, 1), 0.0)
                    dst[jr * 3 + jw, pl.ds(to, 16), :] = z.astype(BF16)
            return 0
        lax.fori_loop(0, cf // 16, step, 0)

    def build_arrived(buf, dst, t):
        for way in range(2):
            @pl.when(arrives(t, way))
            def _():
                shard = f - t if way == 0 else f + t
                build(buf.at[shard], shard * cf, dst)

    def halo(hs, hr, ss, rs, way, n):
        cols = pl.ds(pl.multiple_of(n * TILE, TILE), TILE)
        to = s + 1 if way == 0 else s - 1
        return remote(hs.at[way, :, cols], hr.at[way, :, cols],
                      ss.at[way, n], rs.at[way, n], space=to)

    def convolve(w, src, flip, up, mine, hs, hr, ss, rs):
        def step(n, _):
            cols = pl.ds(pl.multiple_of(n * TILE, TILE), TILE)
            acc = jnp.zeros((3 * cf, TILE), F32)
            for t in range(9):
                wt = jnp.concatenate([w[kd * 9 + t] for kd in range(3)], axis=0)
                acc = acc + jnp.dot(wt, src[8 - t if flip else t, :, cols],
                                    preferred_element_type=F32)
            mine[:, cols] = acc[cf : 2 * cf]
            hs[0, :, cols] = acc[up * cf : (up + 1) * cf]
            hs[1, :, cols] = acc[(2 - up) * cf : (3 - up) * cf]

            @pl.when(s + 1 < S)
            def _():
                halo(hs, hr, ss, rs, 0, n).start()

            @pl.when(s >= 1)
            def _():
                halo(hs, hr, ss, rs, 1, n).start()
            return 0
        lax.fori_loop(0, tiles, step, 0)

    def finish(mine, hs, hr, ss, rs):
        def step(n, _):
            cols = pl.ds(pl.multiple_of(n * TILE, TILE), TILE)

            @pl.when(s >= 1)
            def _():
                halo(hs, hr, ss, rs, 0, n).wait_recv()
                mine[:, cols] += hr[0, :, cols]

            @pl.when(s + 1 < S)
            def _():
                halo(hs, hr, ss, rs, 1, n).wait_recv()
                mine[:, cols] += hr[1, :, cols]

            @pl.when(s + 1 < S)
            def _():
                halo(hs, hr, ss, rs, 0, n).wait_send()

            @pl.when(s >= 1)
            def _():
                halo(hs, hr, ss, rs, 1, n).wait_send()
            return 0
        lax.fori_loop(0, tiles, step, 0)

    start_line(cot_ref, xcot, cot_ss, cot_rs)
    up_halo = remote(in_ref, in3.at[0], halo_ss.at[0], halo_rs.at[0], space=s + 1)
    down_halo = remote(in_ref, in3.at[2], halo_ss.at[1], halo_rs.at[1], space=s - 1)

    @pl.when(s + 1 < S)
    def _():
        up_halo.start()

    @pl.when(s >= 1)
    def _():
        down_halo.start()

    lanes = 128 // cf
    groups = -(-27 // lanes)
    for g in range(groups):
        taps = [min(g + b * groups, 26) for b in range(lanes)]
        x = jnp.concatenate([w_ref[k].astype(F32) for k in taps], axis=0)
        xt = x.T.astype(BF16)
        for to in range(F):
            wst[to, g * cf : (g + 1) * cf, :] = xt[to * cf : (to + 1) * cf]
    wrx[f] = wst[f]
    wrows = groups * cf // Q
    part = lax.rem(s, Q)

    def wpart(ref, shard, q):
        return ref.at[shard, pl.ds(pl.multiple_of(q * wrows, 16), wrows), :]

    def w_first(d):
        to = lax.rem(f + d, F)
        return remote(wpart(wst, to, part), wpart(wrx, f, part), w1_ss.at[d - 1], w1_rs.at[d - 1], filt=to)

    def w_first_in(d):
        frm = lax.rem(f - d + F, F)
        return remote(wpart(wst, frm, part), wpart(wrx, frm, part), w1_ss.at[d - 1], w1_rs.at[d - 1], filt=frm)

    def w_second(d, e):
        frm = lax.rem(f - d + F, F)
        to = (s // Q) * Q + lax.rem(part + e, Q)
        return remote(wpart(wrx, frm, part), wpart(wrx, frm, part),
                      w2_ss.at[d - 1, e - 1], w2_rs.at[d - 1, e - 1], space=to)

    def w_second_in(d, e):
        frm = lax.rem(f - d + F, F)
        q = lax.rem(part - e + Q, Q)
        to = (s // Q) * Q + q
        return remote(wpart(wrx, frm, q), wpart(wrx, frm, q),
                      w2_ss.at[d - 1, e - 1], w2_rs.at[d - 1, e - 1], space=to)

    for d in range(1, F):
        w_first(d).start()

    build(cot_ref, f * cf, s_cot)
    in3[1] = in_ref[...]

    @pl.when(s == 0)
    def _():
        in3[0] = jnp.zeros((cf, plane), BF16)

    @pl.when(s == S - 1)
    def _():
        in3[2] = jnp.zeros((cf, plane), BF16)

    for t in range(1, F):
        relay(cot_ref, xcot, cot_ss, cot_rs, t)
        if t == F - 1:
            start_line(in_ref, xin, in_ss, in_rs)
        build_arrived(xcot, s_cot, t)
        if t == 1:
            for d in range(1, F):
                w_first_in(d).wait_recv()
                for e in range(1, Q):
                    w_second(d, e).start()

    convolve(w_ref, s_cot, False, 2, gi_ref, hs_b, hr_b, hb_ss, hb_rs)
    relay(in_ref, xin, in_ss, in_rs, 1)

    @pl.when(s >= 1)
    def _():
        up_halo.wait_recv()

    @pl.when(s + 1 < S)
    def _():
        down_halo.wait_recv()

    def grads(t, _):
        r = lax.dot_general(in3[...].reshape(3 * cf, plane), s_cot[t], (((1,), (1,)), ((), ())),
                            preferred_element_type=F32)
        for kd in range(3):
            at = pl.multiple_of((kd * 9 + t) * cf, cf)
            for h in range(2):
                grad[h, pl.ds(at, cf), :] = r[kd * cf : (kd + 1) * cf, h * half : (h + 1) * half]
        return 0

    lax.fori_loop(0, 9, grads, 0)
    bsum = jnp.sum(cot_ref[...].astype(F32), axis=1, keepdims=True)
    for h in range(2):
        grad[h, 27 * cf :, :] = jnp.broadcast_to(bsum, (cf, half))
    pair = remote(grad.at[1 - core], gpair, pair_ss, pair_rs, space=partner)
    pair.start()

    build(in_ref, f * cf, s_in)
    build_arrived(xin, s_in, 1)
    for t in range(2, F - 1):
        relay(in_ref, xin, in_ss, in_rs, t)
        if t < F - 2:
            build_arrived(xin, s_in, t)

    pair.wait()
    rows = grad.shape[1]
    chunk = rows // H
    grad[core] += gpair[...]

    def place(ref, h):
        return ref.at[core, pl.ds(pl.multiple_of(h * chunk, 8), chunk), :]

    def scatter(d):
        to = lax.rem(chip + d, H)
        return remote(place(grad, to), grx.at[d - 1], rs_ss.at[d - 1], rs_rs.at[d - 1],
                      space=2 * to + core)

    def spread(d):
        to = lax.rem(chip + d, H)
        return remote(place(gfin, chip), place(gfin, chip), ag_ss.at[d - 1], ag_rs.at[d - 1],
                      space=2 * to + core)

    def spread_in(d):
        frm = lax.rem(chip - d + H, H)
        return remote(place(gfin, frm), place(gfin, frm), ag_ss.at[d - 1], ag_rs.at[d - 1],
                      space=2 * frm + core)

    def local(d):
        frm = lax.rem(chip - d + H, H)
        return remote(place(gfin, frm), place(gfin, frm), lo_ss.at[d], lo_rs.at[d], space=partner)

    def local_in(d):
        frm = lax.rem(chip - d + H, H)
        there = gfin.at[1 - core, pl.ds(pl.multiple_of(frm * chunk, 8), chunk), :]
        return remote(there, there, lo_ss.at[d], lo_rs.at[d], space=partner)

    for d in range(1, H):
        scatter(d).start()

    for d in range(1, F):
        for e in range(1, Q):
            w_second_in(d, e).wait_recv()
    for g in range(groups):
        for b in range(lanes):
            tap = g + b * groups
            if tap < 27:
                wf[tap] = jnp.concatenate(
                    [wrx[k, g * cf : (g + 1) * cf, b * cf : (b + 1) * cf] for k in range(F)], axis=1)
    if F > 3:
        build_arrived(xin, s_in, F - 2)

    for d in range(1, H):
        scatter(d).wait_recv()
    mine_at = pl.ds(pl.multiple_of(chip * chunk, 8), chunk)
    total = grad[core, mine_at, :]
    for d in range(1, H):
        total = total + grx[d - 1]
    gfin[core, mine_at, :] = total * factor
    for d in range(1, H):
        spread(d).start()
    local(0).start()

    relay(in_ref, xin, in_ss, in_rs, F - 1)
    build_arrived(xin, s_in, F - 1)
    convolve(wf, s_in, True, 0, out_ref, hs_f, hr_f, hf_ss, hf_rs)
    finish(gi_ref, hs_b, hr_b, hb_ss, hb_rs)
    for d in range(1, H):
        spread_in(d).wait_recv()
        local(d).start()
    for d in range(H):
        local_in(d).wait_recv()
    for h in range(2):
        gw_ref[:, h * half : (h + 1) * half] = gfin[h, : 27 * cf, :]
    gb_ref[...] = gfin[0, 27 * cf :, :]
    out_ref[...] += bias_ref[...]
    finish(out_ref, hs_f, hr_f, hf_ss, hf_rs)

    end_line(cot_ref, xcot, cot_ss, cot_rs)
    end_line(in_ref, xin, in_ss, in_rs)

    @pl.when(s + 1 < S)
    def _():
        up_halo.wait_send()

    @pl.when(s >= 1)
    def _():
        down_halo.wait_send()

    for d in range(1, F):
        w_first(d).wait_send()
        for e in range(1, Q):
            w_second(d, e).wait_send()
    for d in range(1, H):
        scatter(d).wait_send()
        spread(d).wait_send()
    for d in range(H):
        local(d).wait_send()


def body(F, S, inputs, weight, bias, cotangent):
    planes, cf, plane = inputs.shape
    assert planes == 1
    chans = weight.shape[4]
    H = S // 2
    lanes = 128 // cf
    wrows = -(-27 // lanes) * cf
    Q = S
    while Q > 2 and (wrows % Q or (wrows // Q) % 16):
        Q //= 2
    factor = 1.0 / float(S * plane) ** 0.5
    rows = 28 * cf
    dma = pltpu.SemaphoreType.DMA
    tiles = plane // TILE
    vmem = pl.BlockSpec(memory_space=pltpu.VMEM)
    V = pltpu.VMEM
    out, gi, gw, gb = pl.pallas_call(
        functools.partial(kernel, F, S, Q, factor),
        out_shape=(
            jax.ShapeDtypeStruct((cf, plane), F32),
            jax.ShapeDtypeStruct((cf, plane), F32),
            jax.ShapeDtypeStruct((27 * cf, chans), F32),
            jax.ShapeDtypeStruct((cf, chans // 2), F32),
        ),
        in_specs=[vmem] * 4,
        out_specs=(vmem,) * 4,
        scratch_shapes=[
            V((F, cf, plane), BF16), V((F, cf, plane), BF16), V((3, cf, plane), BF16),
            V((9, chans, plane), BF16), V((9, chans, plane), BF16),
            V((F, wrows, 128), BF16), V((F, wrows, 128), BF16), V((27, cf, chans), BF16),
            V((2, cf, plane), F32), V((2, cf, plane), F32),
            V((2, cf, plane), F32), V((2, cf, plane), F32),
            V((2, rows, chans // 2), F32), V((rows, chans // 2), F32),
            V((H - 1, rows // H, chans // 2), F32), V((2, rows, chans // 2), F32),
            dma((2, F - 1)), dma((2, F - 1)), dma((2, F - 1)), dma((2, F - 1)),
            dma((2,)), dma((2,)),
            dma((F - 1,)), dma((F - 1,)), dma((F - 1, Q - 1)), dma((F - 1, Q - 1)),
            dma((2, tiles)), dma((2, tiles)), dma((2, tiles)), dma((2, tiles)),
            dma, dma, dma((H - 1,)), dma((H - 1,)), dma((H - 1,)), dma((H - 1,)),
            dma((H,)), dma((H,)),
        ],
        compiler_params=pltpu.CompilerParams(
            collective_id=0, has_side_effects=True, vmem_limit_bytes=56 * 1024 * 1024),
        cost_estimate=pl.CostEstimate(
            flops=3 * 2 * 27 * cf * chans * plane, bytes_accessed=8 * 1024 * 1024, transcendentals=0),
    )(
        inputs.reshape(cf, plane),
        weight.reshape(27, cf, chans),
        bias.astype(F32).reshape(cf, 1),
        cotangent.reshape(cf, plane),
    )
    return (
        out.reshape(1, cf, plane),
        gi.reshape(1, cf, plane),
        gw.reshape(3, 3, 3, cf, chans),
        gb[:, 0],
    )


def solution(mesh):
    placed = (
        P("space", "filt", None),
        P(None, None, None, "filt", None),
        P("filt"),
        P("space", "filt", None),
    )
    return jax.shard_map(
        functools.partial(body, mesh.shape["filt"], mesh.shape["space"]),
        mesh=mesh,
        in_specs=placed,
        out_specs=(
            P("space", "filt", None),
            P("space", "filt", None),
            P(None, None, None, "filt", None),
            P("filt"),
        ),
        check_vma=False,
    )
```

profile of v0, /device:TPU:1, one launch (start us, length us, event | category | flops | bytes accessed | tf_op | source)
XLA Modules:
  0.0 87.2 jit_solution(11416095600893806051)
XLA Ops:
  0.6 0.7 bitcast_convert_fusion
  1.3 0.7 copy.9.bias_ref
  2.0 78.7 %shard_map.75 = (f32[64,2048]{1,0:T(8,128)}, f32[64,2048]{1,0:T(8,128)}, f32[1728,256]{1,0:T(8,128)}, f32[64,128]{1,0:T(8,128)}) custom-call(bf16[64,2048]{1,0:T(8,128)(2,1)} %bitcast.13, bf16[27,64,256]{2,1,0:T(8,128)(2,1)} %bitcast.12, f32[64,1]{1,0:T(8,128)} %copy.9.bias_ref, bf16[64,2048]{1,0:T(8,128)(2,1)} %bitcast.14), custom_call_target="tpu_custom_call" | custom-call | flops 5435817984 | bytes 8388608 | tf_op jit(solution)/shard_map/pallas_call | solution.py:399
  80.7 0.0 copy-start
  80.7 1.5 %slice_reduce_fusion = f32[64]{0:T(128)} fusion(f32[64,128]{1,0:T(8,128)} %get-tuple-element.11), kind=kLoop, calls=%fused_computation | loop fusion | bytes 512 | tf_op jit(solution)/shard_map/slice | solution.py:438
  82.2 1.9 %copy.13 = f32[1,64,2048]{2,1,0:T(8,128)} copy(f32[1,64,2048]{2,1,0:T(8,128)} %bitcast.11) | data formatting | bytes 1048576
  84.1 1.9 %copy.14 = f32[1,64,2048]{2,1,0:T(8,128)} copy(f32[1,64,2048]{2,1,0:T(8,128)} %bitcast.10) | data formatting | bytes 1048576
  86.0 0.0 copy-done
  86.0 1.2 %copy.15 = f32[3,3,3,64,256]{4,3,2,1,0:T(8,128)} copy(f32[3,3,3,64,256]{4,3,2,1,0:T(8,128)S(1)} %bitcast.9) | data formatting | bytes 3538944
Async XLA Ops:
  80.7 5.3 %copy-start = (f32[1728,256]{1,0:T(8,128)S(1)}, f32[1728,256]{1,0:T(8,128)}, u32[]{:S(2)}) copy-start(f32[1728,256]{1,0:T(8,128)} %get-tuple-element.10) | copy-start | bytes 5308420
where the time goes:
time: 87.4 us; the launch traced here: 87.2 us
  Pallas kernels  78.7 us (90%)
  local copies, waits for them, and re-layouts  7.18 us (8%)
    pallas_call x1, Pallas kernels, body(): pl.pallas_call(functools.partial(kernel, F, S, Q, factor), out_shape=(jax...  78.7 us
    unnamed x5, local copies, waits for them, and re-layouts  4.95 us

commit v1 on v0

--- a/solution.py
+++ b/solution.py
@@ -40,7 +40,6 @@
     s = lax.axis_index("space")
     cf, plane = in_ref.shape
     chans = w_ref.shape[2]
-    half = chans // 2
     H = S // 2
     core = lax.rem(s, 2)
     chip = s // 2
@@ -76,7 +75,7 @@
             def _():
                 line(own, buf, ss, rs, 1, way).start()
 
-    def relay(own, buf, ss, rs, t):
+    def relay(own, buf, ss, rs, t, follow=False):
         for way in range(2):
             @pl.when(arrives(t, way))
             def _():
@@ -87,6 +86,10 @@
                 @pl.when(sends(t + 1, way))
                 def _():
                     line(own, buf, ss, rs, t + 1, way).start()
+            if follow:
+                @pl.when(jnp.logical_and(sends(1, way), t == (f + 1 if way == 0 else F - f)))
+                def _():
+                    line(in_ref, xin, in_ss, in_rs, 1, way).start()
 
     def end_line(own, buf, ss, rs):
         for way in range(2):
@@ -240,85 +243,130 @@
     def _():
         in3[2] = jnp.zeros((cf, plane), BF16)
 
+    stages = chans // 128
+    rows = grad.shape[1]
+    hrows = rows // 2
+    chunk = hrows // H
+    per_stage = F // stages
+    first = f // per_stage
+
+    def rows_of(c, h):
+        return pl.ds(pl.multiple_of(c * hrows + h * chunk, 8), chunk)
+
+    def pair(g):
+        there = pl.ds(pl.multiple_of((1 - core) * hrows, 8), hrows)
+        return remote(grad.at[g, there, :], gpair.at[g], pair_ss.at[g], pair_rs.at[g], space=partner)
+
+    def scatter(g, d):
+        to = lax.rem(chip + d, H)
+        return remote(grad.at[g, rows_of(core, to), :], grx.at[g, d - 1],
+                      rs_ss.at[g, d - 1], rs_rs.at[g, d - 1], space=2 * to + core)
+
+    def spread(g, d):
+        to = lax.rem(chip + d, H)
+        mine = gfin.at[g, rows_of(core, chip), :]
+        return remote(mine, mine, ag_ss.at[g, d - 1], ag_rs.at[g, d - 1], space=2 * to + core)
+
+    def spread_in(g, d):
+        frm = lax.rem(chip - d + H, H)
+        there = gfin.at[g, rows_of(core, frm), :]
+        return remote(there, there, ag_ss.at[g, d - 1], ag_rs.at[g, d - 1], space=2 * frm + core)
+
+    def local(g, d):
+        frm = lax.rem(chip - d + H, H)
+        there = gfin.at[g, rows_of(core, frm), :]
+        return remote(there, there, lo_ss.at[g, d], lo_rs.at[g, d], space=partner)
+
+    def local_in(g, d):
+        frm = lax.rem(chip - d + H, H)
+        there = gfin.at[g, rows_of(1 - core, frm), :]
+        return remote(there, there, lo_ss.at[g, d], lo_rs.at[g, d], space=partner)
+
+    def grads(g):
+        lanes_at = pl.ds(pl.multiple_of(lax.rem(first + g, stages) * 128, 128), 128)
+
+        def step(t, _):
+            r = lax.dot_general(in3[...].reshape(3 * cf, plane), s_cot[t, lanes_at, :],
+                                (((1,), (1,)), ((), ())), preferred_element_type=F32)
+            for kd in range(3):
+                at = pl.multiple_of((kd * 9 + t) * cf, cf)
+                grad[g, pl.ds(at, cf), :] = r[kd * cf : (kd + 1) * cf]
+            return 0
+
+        lax.fori_loop(0, 9, step, 0)
+        bsum = jnp.sum(cot_ref[...].astype(F32), axis=1, keepdims=True)
+        grad[g, 27 * cf :, :] = jnp.broadcast_to(bsum, (cf, 128))
+        pair(g).start()
+
+    def pair_sum(g):
+        pair(g).wait()
+        here = pl.ds(pl.multiple_of(core * hrows, 8), hrows)
+        grad[g, here, :] += gpair[g]
+        for d in range(1, H):
+            scatter(g, d).start()
+
+    def chunk_sum(g):
+        for d in range(1, H):
+            scatter(g, d).wait_recv()
+        at = rows_of(core, chip)
+        total = grad[g, at, :]
+        for d in range(1, H):
+            total = total + grx[g, d - 1]
+        gfin[g, at, :] = total * factor
+        for d in range(1, H):
+            spread(g, d).start()
+        local(g, 0).start()
+
+    def chunks_in(g):
+        for d in range(1, H):
+            spread_in(g, d).wait_recv()
+            local(g, d).start()
+
+    def write_grad(g):
+        for d in range(H):
+            local_in(g, d).wait_recv()
+        lanes_at = pl.ds(pl.multiple_of(lax.rem(first + g, stages) * 128, 128), 128)
+        gw_ref[:, lanes_at] = gfin[g, : 27 * cf, :]
+
     for t in range(1, F):
-        relay(cot_ref, xcot, cot_ss, cot_rs, t)
+        relay(cot_ref, xcot, cot_ss, cot_rs, t, True)
+        if t == per_stage:
+            pair_sum(0)
         if t == F - 1:
-            start_line(in_ref, xin, in_ss, in_rs)
+            chunk_sum(0)
         build_arrived(xcot, s_cot, t)
+        if t == per_stage - 1:
+            @pl.when(s >= 1)
+            def _():
+                up_halo.wait_recv()
+
+            @pl.when(s + 1 < S)
+            def _():
+                down_halo.wait_recv()
+
+            grads(0)
         if t == 1:
             for d in range(1, F):
                 w_first_in(d).wait_recv()
                 for e in range(1, Q):
                     w_second(d, e).start()
+    for g in range(1, stages):
+        grads(g)
 
     convolve(w_ref, s_cot, False, 2, gi_ref, hs_b, hr_b, hb_ss, hb_rs)
+    for g in range(1, stages):
+        pair_sum(g)
+
     relay(in_ref, xin, in_ss, in_rs, 1)
-
-    @pl.when(s >= 1)
-    def _():
-        up_halo.wait_recv()
-
-    @pl.when(s + 1 < S)
-    def _():
-        down_halo.wait_recv()
-
-    def grads(t, _):
-        r = lax.dot_general(in3[...].reshape(3 * cf, plane), s_cot[t], (((1,), (1,)), ((), ())),
-                            preferred_element_type=F32)
-        for kd in range(3):
-            at = pl.multiple_of((kd * 9 + t) * cf, cf)
-            for h in range(2):
-                grad[h, pl.ds(at, cf), :] = r[kd * cf : (kd + 1) * cf, h * half : (h + 1) * half]
-        return 0
-
-    lax.fori_loop(0, 9, grads, 0)
-    bsum = jnp.sum(cot_ref[...].astype(F32), axis=1, keepdims=True)
-    for h in range(2):
-        grad[h, 27 * cf :, :] = jnp.broadcast_to(bsum, (cf, half))
-    pair = remote(grad.at[1 - core], gpair, pair_ss, pair_rs, space=partner)
-    pair.start()
-
     build(in_ref, f * cf, s_in)
     build_arrived(xin, s_in, 1)
     for t in range(2, F - 1):
         relay(in_ref, xin, in_ss, in_rs, t)
-        if t < F - 2:
-            build_arrived(xin, s_in, t)
-
-    pair.wait()
-    rows = grad.shape[1]
-    chunk = rows // H
-    grad[core] += gpair[...]
-
-    def place(ref, h):
-        return ref.at[core, pl.ds(pl.multiple_of(h * chunk, 8), chunk), :]
-
-    def scatter(d):
-        to = lax.rem(chip + d, H)
-        return remote(place(grad, to), grx.at[d - 1], rs_ss.at[d - 1], rs_rs.at[d - 1],
-                      space=2 * to + core)
-
-    def spread(d):
-        to = lax.rem(chip + d, H)
-        return remote(place(gfin, chip), place(gfin, chip), ag_ss.at[d - 1], ag_rs.at[d - 1],
-                      space=2 * to + core)
-
-    def spread_in(d):
-        frm = lax.rem(chip - d + H, H)
-        return remote(place(gfin, frm), place(gfin, frm), ag_ss.at[d - 1], ag_rs.at[d - 1],
-                      space=2 * frm + core)
-
-    def local(d):
-        frm = lax.rem(chip - d + H, H)
-        return remote(place(gfin, frm), place(gfin, frm), lo_ss.at[d], lo_rs.at[d], space=partner)
-
-    def local_in(d):
-        frm = lax.rem(chip - d + H, H)
-        there = gfin.at[1 - core, pl.ds(pl.multiple_of(frm * chunk, 8), chunk), :]
-        return remote(there, there, lo_ss.at[d], lo_rs.at[d], space=partner)
-
-    for d in range(1, H):
-        scatter(d).start()
+        if t == 2:
+            chunks_in(0)
+        build_arrived(xin, s_in, t)
+    for g in range(1, stages):
+        chunk_sum(g)
 
     for d in range(1, F):
         for e in range(1, Q):
@@ -329,33 +377,18 @@
             if tap < 27:
                 wf[tap] = jnp.concatenate(
                     [wrx[k, g * cf : (g + 1) * cf, b * cf : (b + 1) * cf] for k in range(F)], axis=1)
-    if F > 3:
-        build_arrived(xin, s_in, F - 2)
-
-    for d in range(1, H):
-        scatter(d).wait_recv()
-    mine_at = pl.ds(pl.multiple_of(chip * chunk, 8), chunk)
-    total = grad[core, mine_at, :]
-    for d in range(1, H):
-        total = total + grx[d - 1]
-    gfin[core, mine_at, :] = total * factor
-    for d in range(1, H):
-        spread(d).start()
-    local(0).start()
 
     relay(in_ref, xin, in_ss, in_rs, F - 1)
     build_arrived(xin, s_in, F - 1)
     convolve(wf, s_in, True, 0, out_ref, hs_f, hr_f, hf_ss, hf_rs)
+    for g in range(1, stages):
+        chunks_in(g)
     finish(gi_ref, hs_b, hr_b, hb_ss, hb_rs)
-    for d in range(1, H):
-        spread_in(d).wait_recv()
-        local(d).start()
-    for d in range(H):
-        local_in(d).wait_recv()
-    for h in range(2):
-        gw_ref[:, h * half : (h + 1) * half] = gfin[h, : 27 * cf, :]
-    gb_ref[...] = gfin[0, 27 * cf :, :]
-    out_ref[...] += bias_ref[...]
+    write_grad(0)
+    out_ref[...] += jnp.broadcast_to(bias_ref[...].astype(F32), (128, cf)).T[:, :1]
+    for g in range(1, stages):
+        write_grad(g)
+    gb_ref[...] = gfin[0, 27 * cf :, :].T[:1, :]
     finish(out_ref, hs_f, hr_f, hf_ss, hf_rs)
 
     end_line(cot_ref, xcot, cot_ss, cot_rs)
@@ -373,11 +406,12 @@
         w_first(d).wait_send()
         for e in range(1, Q):
             w_second(d, e).wait_send()
-    for d in range(1, H):
-        scatter(d).wait_send()
-        spread(d).wait_send()
-    for d in range(H):
-        local(d).wait_send()
+    for g in range(stages):
+        for d in range(1, H):
+            scatter(g, d).wait_send()
+            spread(g, d).wait_send()
+        for d in range(H):
+            local(g, d).wait_send()
 
 
 def body(F, S, inputs, weight, bias, cotangent):
@@ -387,9 +421,8 @@
     H = S // 2
     lanes = 128 // cf
     wrows = -(-27 // lanes) * cf
-    Q = S
-    while Q > 2 and (wrows % Q or (wrows // Q) % 16):
-        Q //= 2
+    Q = 2
+    stages = chans // 128
     factor = 1.0 / float(S * plane) ** 0.5
     rows = 28 * cf
     dma = pltpu.SemaphoreType.DMA
@@ -402,7 +435,7 @@
             jax.ShapeDtypeStruct((cf, plane), F32),
             jax.ShapeDtypeStruct((cf, plane), F32),
             jax.ShapeDtypeStruct((27 * cf, chans), F32),
-            jax.ShapeDtypeStruct((cf, chans // 2), F32),
+            jax.ShapeDtypeStruct((1, cf), F32),
         ),
         in_specs=[vmem] * 4,
         out_specs=(vmem,) * 4,
@@ -412,14 +445,14 @@
             V((F, wrows, 128), BF16), V((F, wrows, 128), BF16), V((27, cf, chans), BF16),
             V((2, cf, plane), F32), V((2, cf, plane), F32),
             V((2, cf, plane), F32), V((2, cf, plane), F32),
-            V((2, rows, chans // 2), F32), V((rows, chans // 2), F32),
-            V((H - 1, rows // H, chans // 2), F32), V((2, rows, chans // 2), F32),
+            V((stages, rows, 128), F32), V((stages, rows // 2, 128), F32),
+            V((stages, H - 1, rows // (2 * H), 128), F32), V((stages, rows, 128), F32),
             dma((2, F - 1)), dma((2, F - 1)), dma((2, F - 1)), dma((2, F - 1)),
             dma((2,)), dma((2,)),
             dma((F - 1,)), dma((F - 1,)), dma((F - 1, Q - 1)), dma((F - 1, Q - 1)),
             dma((2, tiles)), dma((2, tiles)), dma((2, tiles)), dma((2, tiles)),
-            dma, dma, dma((H - 1,)), dma((H - 1,)), dma((H - 1,)), dma((H - 1,)),
-            dma((H,)), dma((H,)),
+            dma((stages,)), dma((stages,)), dma((stages, H - 1)), dma((stages, H - 1)),
+            dma((stages, H - 1)), dma((stages, H - 1)), dma((stages, H)), dma((stages, H)),
         ],
         compiler_params=pltpu.CompilerParams(
             collective_id=0, has_side_effects=True, vmem_limit_bytes=56 * 1024 * 1024),
@@ -428,14 +461,14 @@
     )(
         inputs.reshape(cf, plane),
         weight.reshape(27, cf, chans),
-        bias.astype(F32).reshape(cf, 1),
+        bias.reshape(1, cf),
         cotangent.reshape(cf, plane),
     )
     return (
         out.reshape(1, cf, plane),
         gi.reshape(1, cf, plane),
         gw.reshape(3, 3, 3, cf, chans),
-        gb[:, 0],
+        gb.reshape(cf),
     )
 
 

time: 87.4 us -> 84 us (0.961)
  Pallas kernels: 78.7 us -> 76.7 us
  local copies, waits for them, and re-layouts: 7.18 us -> 5.6 us
    pallas_call x1, Pallas kernels: 78.7 us -> 76.7 us  [body(): pl.pallas_call(functools.partial(kernel, F, S, Q, factor), out_shape=(jax...]
    slice x1 -> x0, local copies, waits for them, and re-layouts: 1.51 us -> none  [body(): gb[:, 0]]
    unnamed x5 -> x8, local copies, waits for them, and re-layouts: 4.95 us -> 5.6 us
where the time goes in v1:
time: 84 us; the launch traced here: 82.9 us
  Pallas kernels  76.7 us (91%)
  local copies, waits for them, and re-layouts  5.6 us (7%)
    pallas_call x1, Pallas kernels, body(): pl.pallas_call(functools.partial(kernel, F, S, Q, factor), out_shape=(jax...  76.7 us
    unnamed x8, local copies, waits for them, and re-layouts  5.6 us

profile of v1, /device:TPU:1, one launch (start us, length us, event | category | flops | bytes accessed | tf_op | source)
XLA Modules:
  0.0 82.9 jit_solution(3555484139787341468)
XLA Ops:
  0.6 76.7 %shard_map.75 = (f32[64,2048]{1,0:T(8,128)}, f32[64,2048]{1,0:T(8,128)}, f32[1728,256]{1,0:T(8,128)}, f32[1,64]{1,0:T(1,128)}) custom-call(bf16[64,2048]{1,0:T(8,128)(2,1)} %bitcast.12, bf16[27,64,256]{2,1,0:T(8,128)(2,1)} %bitcast.11, bf16[1,64]{1,0:T(2,128)(2,1)} %bitcast.14, bf16[64,2048]{1,0:T(8,128)(2,1)} %bitcast.13), custom_call_target="tpu_custom_call" | custom-call | flops 5435817984 | bytes 8388608 | tf_op jit(solution)/shard_map/pallas_call | solution.py:432
  77.3 0.0 copy-start
  77.3 2.0 %copy.12 = f32[1,64,2048]{2,1,0:T(8,128)} copy(f32[1,64,2048]{2,1,0:T(8,128)} %bitcast.10) | data formatting | bytes 1048576
  79.3 1.9 %copy.13 = f32[1,64,2048]{2,1,0:T(8,128)} copy(f32[1,64,2048]{2,1,0:T(8,128)} %bitcast.9) | data formatting | bytes 1048576
  81.2 0.0 copy-done
  81.2 0.0 copy-start.1
  81.2 1.2 %copy.14 = f32[3,3,3,64,256]{4,3,2,1,0:T(8,128)} copy(f32[3,3,3,64,256]{4,3,2,1,0:T(8,128)S(1)} %bitcast.8) | data formatting | bytes 3538944
  82.4 0.0 copy-done.1
  82.4 0.5 copy.15
Async XLA Ops:
  77.3 3.9 %copy-start = (f32[1728,256]{1,0:T(8,128)S(1)}, f32[1728,256]{1,0:T(8,128)}, u32[]{:S(2)}) copy-start(f32[1728,256]{1,0:T(8,128)} %get-tuple-element.10) | copy-start | bytes 5308420
  81.2 1.2 %copy-start.1 = (f32[1,64]{1,0:T(1,128)S(1)}, f32[1,64]{1,0:T(1,128)}, u32[]{:S(2)}) copy-start(f32[1,64]{1,0:T(1,128)} %get-tuple-element.11) | copy-start | bytes 772

commit v2 on v1

--- a/solution.py
+++ b/solution.py
@@ -350,14 +350,13 @@
                 w_first_in(d).wait_recv()
                 for e in range(1, Q):
                     w_second(d, e).start()
+    convolve(w_ref, s_cot, False, 2, gi_ref, hs_b, hr_b, hb_ss, hb_rs)
     for g in range(1, stages):
         grads(g)
-
-    convolve(w_ref, s_cot, False, 2, gi_ref, hs_b, hr_b, hb_ss, hb_rs)
+    relay(in_ref, xin, in_ss, in_rs, 1)
     for g in range(1, stages):
         pair_sum(g)
 
-    relay(in_ref, xin, in_ss, in_rs, 1)
     build(in_ref, f * cf, s_in)
     build_arrived(xin, s_in, 1)
     for t in range(2, F - 1):
@@ -421,7 +420,9 @@
     H = S // 2
     lanes = 128 // cf
     wrows = -(-27 // lanes) * cf
-    Q = 2
+    Q = S
+    while Q > 2 and (wrows % Q or (wrows // Q) % 16):
+        Q //= 2
     stages = chans // 128
     factor = 1.0 / float(S * plane) ** 0.5
     rows = 28 * cf

time: 84 us -> 79.5 us (0.946)
  Pallas kernels: 76.7 us -> 72.1 us
    pallas_call x1, Pallas kernels: 76.7 us -> 72.1 us  [body(): pl.pallas_call(functools.partial(kernel, F, S, Q, factor), out_shape=(jax...]
where the time goes in v2:
time: 79.5 us; the launch traced here: 78.3 us
  Pallas kernels  72.1 us (91%)
  local copies, waits for them, and re-layouts  5.6 us (7%)
    pallas_call x1, Pallas kernels, body(): pl.pallas_call(functools.partial(kernel, F, S, Q, factor), out_shape=(jax...  72.1 us
    unnamed x8, local copies, waits for them, and re-layouts  5.6 us

profile of v2, /device:TPU:1, one launch (start us, length us, event | category | flops | bytes accessed | tf_op | source)
XLA Modules:
  0.0 78.3 jit_solution(17570445097285793966)
XLA Ops:
  0.6 72.1 %shard_map.75 = (f32[64,2048]{1,0:T(8,128)}, f32[64,2048]{1,0:T(8,128)}, f32[1728,256]{1,0:T(8,128)}, f32[1,64]{1,0:T(1,128)}) custom-call(bf16[64,2048]{1,0:T(8,128)(2,1)} %bitcast.12, bf16[27,64,256]{2,1,0:T(8,128)(2,1)} %bitcast.11, bf16[1,64]{1,0:T(2,128)(2,1)} %bitcast.14, bf16[64,2048]{1,0:T(8,128)(2,1)} %bitcast.13), custom_call_target="tpu_custom_call" | custom-call | flops 5435817984 | bytes 8388608 | tf_op jit(solution)/shard_map/pallas_call | solution.py:433
  72.7 0.0 copy-start
  72.7 2.0 %copy.12 = f32[1,64,2048]{2,1,0:T(8,128)} copy(f32[1,64,2048]{2,1,0:T(8,128)} %bitcast.10) | data formatting | bytes 1048576
  74.7 1.9 %copy.13 = f32[1,64,2048]{2,1,0:T(8,128)} copy(f32[1,64,2048]{2,1,0:T(8,128)} %bitcast.9) | data formatting | bytes 1048576
  76.6 0.0 copy-done
  76.6 0.0 copy-start.1
  76.6 1.2 %copy.14 = f32[3,3,3,64,256]{4,3,2,1,0:T(8,128)} copy(f32[3,3,3,64,256]{4,3,2,1,0:T(8,128)S(1)} %bitcast.8) | data formatting | bytes 3538944
  77.8 0.0 copy-done.1
  77.8 0.5 copy.15
Async XLA Ops:
  72.7 3.9 %copy-start = (f32[1728,256]{1,0:T(8,128)S(1)}, f32[1728,256]{1,0:T(8,128)}, u32[]{:S(2)}) copy-start(f32[1728,256]{1,0:T(8,128)} %get-tuple-element.10) | copy-start | bytes 5308420
  76.6 1.2 %copy-start.1 = (f32[1,64]{1,0:T(1,128)S(1)}, f32[1,64]{1,0:T(1,128)}, u32[]{:S(2)}) copy-start(f32[1,64]{1,0:T(1,128)} %get-tuple-element.11) | copy-start | bytes 772
